TPU v7x, 128 devices: a whole 4x4x4 slice. The times are simulated.
128 devices in a mesh: pair: 8 (over y, core), slab: 16 (over x, z).
Axes of the slice: x: 4, y: 4, z: 4, core: 2. Of those that a mesh axis runs over, the one named last changes fastest.
Arguments:
- amplitudes: bfloat16 [16, 1536, 1536], P('slab', 'pair'), may hold values from -6 to 6
- integrals: bfloat16 [16, 1536, 1536], P('slab', 'pair'), may hold values from -0.4375 to 0.4375
- occ_slab: int32 [16], P('slab'), may hold values from 0 to 7
- occ_inner: int32 [1], replicated, may hold values from 0 to 7
- occ_outer: int32 [16], replicated, may hold values from 0 to 7
- vir_offset: int32 [9], replicated, may hold values from 0 to 1536, as said below
- residual: bfloat16 [16, 1536, 24576], P('slab', 'pair'), may hold values from -6 to 6
Outputs:
- updated: bfloat16 [16, 1536, 24576], P('slab', 'pair')
Inputs may be any that keep to these rules, and one draw needn't show every extreme that they name: vir_offset[0] is 0, vir_offset[8] is 1536, and the entries rise strictly.
All inputs are finite; a program needn't handle non-finite values.
Results may differ from a plain program's by a relative error of at most 0.001.
Values may be sent and summed in bfloat16 or wider, within the bound.
No kernel may reach another device: no remote copies, remote signals or barrier semaphores. Data moves between devices by JAX's collectives and lax.ppermute only.
A program may use at most 128 MiB of HBM per device.

v0:
```python
import jax
import jax.numpy as jnp
from jax import lax
from jax.sharding import PartitionSpec as P

V = 1536


def vir_labels(vir_offset, count):
    position = jnp.arange(count, dtype=jnp.int32)
    return jnp.sum((position[:, None] >= vir_offset[None, 1:8]).astype(jnp.int32), axis=1)


def mask_block(block, row_labels, col_labels, k_labels):
    keep = (
        jnp.bitwise_xor(
            jnp.bitwise_xor(row_labels[:, None, None], col_labels[None, :, None]),
            k_labels[None, None, :],
        )
        == 0
    )
    return block * keep.astype(block.dtype)


def per_device(amplitudes, integrals, occ_slab, occ_inner, occ_outer, vir_offset, residual):
    labels = vir_labels(vir_offset, V)
    k_labels = jnp.bitwise_xor(occ_inner[:, None], labels[None, :]).reshape(-1)
    pair_width = integrals.shape[1]
    own_labels = lax.dynamic_slice_in_dim(labels, lax.axis_index("pair") * pair_width, pair_width)
    rows_here = amplitudes.shape[0]
    outer_count = occ_outer.shape[0]
    whole_amps = lax.all_gather(amplitudes, "pair", axis=1, tiled=True)
    masked_amps = mask_block(whole_amps, occ_slab, labels, k_labels)
    weights = mask_block(
        lax.all_gather(integrals, "slab", axis=0, tiled=True), occ_outer, own_labels, k_labels
    )
    cycle = jnp.einsum("iak,jbk->ibja", masked_amps, weights, preferred_element_type=jnp.float32)
    cycle = cycle.reshape(rows_here, pair_width, outer_count * V)
    return (residual.astype(jnp.float32) + cycle).astype(jnp.bfloat16)


def solution(mesh):
    placed = (
        P("slab", "pair", None),
        P("slab", "pair", None),
        P("slab"),
        P(),
        P(),
        P(),
        P("slab", "pair", None),
    )
    return jax.shard_map(
        per_device, mesh=mesh, in_specs=placed, out_specs=P("slab", "pair", None), check_vma=False
    )
```

profile of v0, /device:TPU:28, one launch (start us, length us, event | category | flops | bytes accessed | tf_op | source)
XLA Modules:
  0.0 166.3 jit_solution(17251748938540070569)
XLA Ops:
  6.5 0.0 all-gather.5.cloned.1.call-start
  6.5 0.7 all-gather.5.cloned.1.call-update
  7.3 0.0 all-gather.3.cloned.1.call-start
  7.3 0.7 all-gather.3.cloned.1.call-update
  9.3 0.7 slice.3
  10.0 0.1 convert_reduce_fusion
  10.1 0.1 dynamic_slice.3
  10.2 0.7 broadcast_xor_fusion
  10.9 32.6 %all-gather.5.cloned.1.call-done = bf16[1,1536,1536]{2,1,0:T(8,128)(2,1)} async-done(((bf16[1,192,1536]{2,1,0:T(8,128)(2,1)}), bf16[1,1536,1536]{2,1,0:T(8,128)(2,1)}) %all-gather.5.cloned.1.call-update) | async-done | bytes 4718608 | tf_op jit(solution)/shard_map/all_gather | solution.py:32
  43.6 79.9 %all-gather.3.cloned.1.call-done = bf16[16,192,1536]{2,1,0:T(8,128)(2,1)} async-done(((bf16[1,192,1536]{2,1,0:T(8,128)(2,1)}), bf16[16,192,1536]{2,1,0:T(8,128)(2,1)}) %all-gather.3.cloned.1.call-update) | async-done | bytes 9437200 | tf_op jit(solution)/shard_map/all_gather | solution.py:35
  123.5 21.7 %fusion.7 = f32[1,16,24,8,1536]{4,3,2,1,0:T(8,128)} fusion(bf16[16,192,1536]{2,1,0:T(8,128)(2,1)} %all-gather.3.cloned.1.call-done, s32[1536]{0:T(1024)S(1)} %get-tuple-element.6, s32[16,192]{1,0:T(8,128)S(1)} %broadcast_xor_fusion, bf16[1,1536,1536]{2,1,0:T(8,128)(2,1)} %all-gather.5.cloned.1.call-done, s32[1536]{0:T(1024)S(1)} %get-tuple-element.5), kind=kOutput, calls=%fused_computation.9 | convolution fusion | flops 14516748288 | bytes 33054720 | tf_op jit(solution)/shard_map/iak,jbk->ibja/dot_general | solution.py:37
  145.2 0.0 copy-start
  145.2 7.3 %copy.11 = f32[1,16,24,8,1536]{4,3,1,2,0:T(8,128)S(1)} copy(f32[1,16,24,8,1536]{4,3,2,1,0:T(8,128)} %fusion.7) | data formatting | bytes 37748736 | tf_op jit(solution)/shard_map/reshape | solution.py:38
  152.6 1.8 %copy-done = bf16[1,192,24576]{2,1,0:T(8,128)(2,1)S(1)} copy-done((bf16[1,192,24576]{2,1,0:T(8,128)(2,1)S(1)}, bf16[1,192,24576]{2,1,0:T(8,128)(2,1)}, u32[]{:S(2)}) %copy-start) | copy-done | bytes 9437208
  154.3 5.1 %add_convert_fusion = bf16[1,192,24576]{2,1,0:T(8,128)(2,1)} fusion(f32[1,192,24576]{2,1,0:T(8,128)S(1)} %bitcast.14, bf16[1,192,24576]{2,1,0:T(8,128)(2,1)S(1)} %copy-done), kind=kLoop, calls=%fused_computation | loop fusion | flops 14155776 | bytes 37748736 | tf_op jit(solution)/shard_map/convert_element_type | solution.py:39
  (1 shorter events, 0.0 us)
Async XLA Ops:
  6.5 37.0 %all-gather.5.cloned.1.call-start = ((), (), s32[]{:S(2)}) async-start(), calls=%async_computation.1 | async-start | bytes 5308416 | tf_op jit(solution)/shard_map/all_gather | solution.py:32
  7.3 116.2 %all-gather.3.cloned.1.call-start = ((), (), s32[]{:S(2)}) async-start(), calls=%async_computation | async-start | bytes 10027008 | tf_op jit(solution)/shard_map/all_gather | solution.py:35
  145.2 9.1 %copy-start = (bf16[1,192,24576]{2,1,0:T(8,128)(2,1)S(1)}, bf16[1,192,24576]{2,1,0:T(8,128)(2,1)}, u32[]{:S(2)}) copy-start(bf16[1,192,24576]{2,1,0:T(8,128)(2,1)} %param.13) | copy-start | bytes 28311556
Sparse Core Ops, SparseCore 0:
  9.0 34.4 all-gather.4
  45.7 77.7 all-gather.2
where the time goes:
time: 168 us; the launch traced here: 166 us
  waiting for transfers between devices  114 us (68%)
  matrix products  21.7 us (13%)
  between operations  14.7 us (9%)
  local copies, waits for them, and re-layouts  9.93 us (6%)
  other arithmetic  5.92 us (4%)
    all_gather x1, waiting for transfers between devices, per_device(): lax.all_gather(integrals, 'slab', axis=0, tiled=True)  79.9 us
    all_gather x1, waiting for transfers between devices, per_device(): whole_amps = lax.all_gather(amplitudes, 'pair', axis=1, tiled=True)  32.6 us
    dot_general x1, matrix products, per_device(): jnp.einsum('iak,jbk->ibja', masked_amps, weights, preferred_element_type=...  21.7 us
    reshape x1, local copies, waits for them, and re-layouts, per_device(): cycle = cycle.reshape(rows_here, pair_width, outer_count * V)  7.34 us
    convert_element_type x1, other arithmetic, per_device(): return (residual.astype(jnp.float32) + cycle).astype(jnp.bfloat16)  5.1 us
  transfers between devices with their start and end apart: 2, of which 2 were waited for; matrix products, arithmetic and copies ran while one was open for 1% of the time, Pallas kernels for 0%

commit v1 on v0

v1 whole, which is shorter than its diff:
```python
import functools

import jax
import jax.numpy as jnp
from jax import lax
from jax.experimental import pallas as pl
from jax.experimental.pallas import tpu as pltpu
from jax.sharding import Mesh, PartitionSpec as P

V = 1536
J = 16
TILE = 256
STEPS = (0, 3, 1, 2)
WIDTHS = (512, 768, 1536)
PLACES = (0, 1, 2)
VMEM_LIMIT = 16 * 1024 * 1024


def labels_at(position, offsets):
    total = jnp.zeros(position.shape, jnp.int32)
    for k in range(1, 8):
        total = total + (position >= offsets[k]).astype(jnp.int32)
    return total


def fold(width, rows, source, out, where, code, offsets):
    block = 32
    col = labels_at(lax.broadcasted_iota(jnp.int32, (1, V), 1), offsets)

    def step(n, carry):
        start = pl.multiple_of(n * block, block)
        here = lax.broadcasted_iota(jnp.int32, (block, 1), 0) + (where[0] + rows + start)
        want = jnp.bitwise_xor(labels_at(here, offsets), code)
        folded = None
        for left in range(0, V, width):
            size = min(width, V - left)
            cut = slice(left, left + size)
            part = source[pl.ds(rows + start, block), cut].astype(jnp.float32)
            part = jnp.where(want == col[:, cut], part, 0.0)
            if size < width:
                part = jnp.concatenate([part, jnp.zeros((block, width - size), jnp.float32)], axis=1)
            folded = part if folded is None else folded + part
        out[pl.ds(start, block), :] = folded.astype(jnp.bfloat16)
        return carry

    lax.fori_loop(0, out.shape[0] // block, step, 0)


def fold_kernel(width, where, offsets, inner, slab, outer, amps, ints, low, high, out):
    code = jnp.bitwise_xor(outer[where[1]], inner[0])
    fold(width, 0, ints, low, where, code, offsets)
    fold(width, low.shape[0], ints, high, where, code, offsets)
    code = jnp.bitwise_xor(slab[0], inner[0])
    fold(width, 0, amps, out, where, code, offsets)


def stage_kernel(source, out, sem):
    copy = pltpu.make_async_copy(source, out, sem)
    copy.start()
    copy.wait()


def flip_kernel(source, out):
    out[...] = source[...].T


def flip(amps):
    vmem = pl.BlockSpec(memory_space=pltpu.VMEM)
    return pl.pallas_call(
        flip_kernel,
        out_shape=jax.ShapeDtypeStruct(amps.shape[::-1], amps.dtype),
        in_specs=[vmem],
        out_specs=vmem,
        compiler_params=pltpu.CompilerParams(vmem_limit_bytes=VMEM_LIMIT),
        name="flip",
    )(amps)


def stage(residual):
    return pl.pallas_call(
        stage_kernel,
        out_shape=jax.ShapeDtypeStruct(residual.shape, residual.dtype),
        in_specs=[pl.BlockSpec(memory_space=pl.ANY)],
        out_specs=pl.BlockSpec(memory_space=pltpu.VMEM),
        scratch_shapes=[pltpu.SemaphoreType.DMA],
        compiler_params=pltpu.CompilerParams(vmem_limit_bytes=VMEM_LIMIT),
        name="stage",
    )(residual)


def cycle_kernel(parts, tiles, where, offsets, slab, outer, amps, *refs):
    pieces = refs[: len(parts)]
    res = refs[len(parts)]
    out_hbm, held, rows_seen, cols_seen, sem = refs[-5:]
    half = held.shape[2]
    x, z = where[2], where[3]
    rows_seen[...] = labels_at(
        where[0] + lax.broadcasted_iota(jnp.int32, rows_seen.shape, 0), offsets
    )
    cols_seen[...] = labels_at(lax.broadcasted_iota(jnp.int32, cols_seen.shape, 1), offsets)
    stores = []
    for n, (low, far) in enumerate(parts):
        own = slice(0, half) if low else slice(half, 2 * half)
        js = []
        for near in STEPS:
            dx, dz = (near, far) if low else (far, near)
            js.append(lax.rem(x + dx, 4) * 4 + lax.rem(z + dz, 4))
        wants = [
            jnp.bitwise_xor(rows_seen[own, :], jnp.bitwise_xor(slab[0], outer[j])) for j in js
        ]

        def tile(start):
            cut = pl.ds(start, TILE)
            cycle = jnp.dot(pieces[n][...], amps[:, cut], preferred_element_type=jnp.float32)
            cols = cols_seen[0:1, cut]
            for s in range(4):
                want = jnp.concatenate([wants[s]] * (TILE // 128), axis=1)
                term = jnp.where(want == cols, cycle[s * half : (s + 1) * half], 0.0)
                here = pl.ds(pl.multiple_of(js[s] * V + start, TILE), TILE)
                held[n, s, :, cut] = (res[own, here].astype(jnp.float32) + term).astype(
                    jnp.bfloat16
                )

        def group(g, carry):
            for t in range(tiles):
                tile(pl.multiple_of(g * (tiles * TILE), TILE) + t * TILE)
            return carry

        if tiles * TILE == V:
            for t in range(tiles):
                tile(t * TILE)
        else:
            lax.fori_loop(0, V // (tiles * TILE), group, 0)
        for s in range(4):
            place = own, pl.ds(pl.multiple_of(js[s] * V, V), V)
            store = pltpu.make_async_copy(held.at[n, s], out_hbm.at[place], sem.at[n, s])
            store.start()
            stores.append(store)
    for store in stores:
        store.wait()


def add_cycle(parts, scalars, amps, pieces, residual, out):
    smem = pl.BlockSpec(memory_space=pltpu.SMEM)
    vmem = pl.BlockSpec(memory_space=pltpu.VMEM)
    hbm = pl.BlockSpec(memory_space=pl.ANY)
    rows = residual.shape[0]
    width = amps.shape[0]
    half = rows // 2
    count = len(parts)
    before = () if out is None else (out,)
    operands = (*scalars, amps, *pieces, residual, *before)
    return pl.pallas_call(
        functools.partial(cycle_kernel, parts, 6 if width < V else 1),
        out_shape=jax.ShapeDtypeStruct(residual.shape, jnp.bfloat16),
        in_specs=[smem] * 4 + [vmem] * (2 + count) + [hbm] * len(before),
        out_specs=hbm,
        scratch_shapes=[
            pltpu.VMEM((count, 4, half, V), jnp.bfloat16),
            pltpu.VMEM((rows, 128), jnp.int32),
            pltpu.VMEM((8, V), jnp.int32),
            pltpu.SemaphoreType.DMA((count, 4)),
        ],
        input_output_aliases={} if out is None else {len(operands) - 1: 0},
        compiler_params=pltpu.CompilerParams(vmem_limit_bytes=VMEM_LIMIT),
        cost_estimate=pl.CostEstimate(
            flops=8 * count * half * V * width,
            bytes_accessed=16 * count * half * V,
            transcendentals=0,
        ),
        name="add_cycle",
    )(*operands)


def ring(shift):
    return [(k, (k + shift) % 4) for k in range(4)]


def neighbours(low, low_axis, high, high_axis):
    got = []
    for shift in (1, 3, 2):
        got.append(lax.ppermute(low, low_axis, ring(shift)))
        got.append(lax.ppermute(high, high_axis, ring(shift)))
    return got[0::2], got[1::2]


def branch(width, where, offsets, inner, slab, outer, amplitudes, integrals, residual):
    rows = amplitudes.shape[0]
    half = rows // 2
    smem = pl.BlockSpec(memory_space=pltpu.SMEM)
    vmem = pl.BlockSpec(memory_space=pltpu.VMEM)
    low, high, amp_folded = pl.pallas_call(
        functools.partial(fold_kernel, width),
        out_shape=[
            jax.ShapeDtypeStruct((n, width), jnp.bfloat16) for n in (half, half, rows)
        ],
        in_specs=[smem] * 5 + [vmem] * 2,
        out_specs=[vmem] * 3,
        compiler_params=pltpu.CompilerParams(vmem_limit_bytes=VMEM_LIMIT),
        name="fold",
    )(where, offsets, inner, slab, outer, amplitudes, integrals)
    amps = flip(lax.all_gather(amp_folded, ("y", "core"), axis=0, tiled=True))

    low_near, high_near = lax.optimization_barrier(neighbours(low, "x", high, "z"))
    amps, residual = lax.optimization_barrier((amps, residual))
    residual = stage(residual)
    low4 = jnp.concatenate([low, *low_near], axis=0)
    high4 = jnp.concatenate([high, *high_near], axis=0)
    low_far, high_far = neighbours(low4, "z", high4, "x")

    scalars = (where, offsets, slab, outer)
    parts = ((True, 0), (False, 0), (False, 2), (False, 1))
    pieces = (low4, high4, high_far[2], high_far[1])
    out = add_cycle(parts, scalars, amps, pieces, residual, None)
    parts = ((False, 3), (True, 2), (True, 1), (True, 3))
    pieces = (high_far[0], low_far[2], low_far[1], low_far[0])
    return add_cycle(parts, scalars, amps, pieces, residual, out)


def per_device(amplitudes, integrals, occ_slab, occ_inner, occ_outer, vir_offset, residual):
    rows = integrals.shape[1]
    x, z = lax.axis_index("x"), lax.axis_index("z")
    pair = lax.axis_index("y") * 2 + lax.axis_index("core")
    where = jnp.stack([pair * rows, x * 4 + z, x, z]).astype(jnp.int32)
    widest = jnp.max(vir_offset[1:] - vir_offset[:-1])
    order = sum((widest > w).astype(jnp.int32) for w in WIDTHS[:-1])
    choice = jnp.int32(PLACES[-1])
    for k, place in enumerate(PLACES[:-1]):
        choice = jnp.where(order == k, place, choice)
    out = lax.switch(
        choice,
        [functools.partial(branch, WIDTHS[PLACES.index(k)]) for k in range(len(WIDTHS))],
        where,
        vir_offset,
        occ_inner,
        occ_slab,
        occ_outer,
        amplitudes[0],
        integrals[0],
        residual[0],
    )
    return out[None]


def solution(mesh):
    fine = Mesh(mesh.devices.reshape(4, 2, 4, 4), ("y", "core", "x", "z"))
    block = P(("x", "z"), ("y", "core"), None)
    placed = (block, block, P(("x", "z")), P(), P(), P(), block)
    return jax.shard_map(
        per_device, mesh=fine, in_specs=placed, out_specs=block, check_vma=False
    )
```

time: 168 us -> 85.8 us (0.51)
  waiting for transfers between devices: 114 us -> 14.7 us
  starting transfers between devices: 0.04 us -> 30.2 us
  Pallas kernels: 0 us -> 22 us
  matrix products: 21.7 us -> 0 us
  local copies, waits for them, and re-layouts: 9.93 us -> 1.77 us
  other arithmetic: 5.92 us -> 1.51 us
    all_gather x2 -> x1, waiting for transfers between devices: 113 us -> 0.01 us  [branch(): amps = flip(lax.all_gather(amp_folded, ('y', 'core'), axis=0, tiled=True))]
    ppermute x0 -> x12, starting transfers between devices: none -> 30.1 us  [the longest x6 22.5 us: neighbours(): got.append(lax.ppermute(high, high_axis, ring(shift)))]
    pallas_call x0 -> x5, Pallas kernels: none -> 22 us  [the longest x2 13.8 us: add_cycle(): pl.pallas_call(functools.partial(cycle_kernel, parts, 6 if width < V else...]
    dot_general x1 -> x0, matrix products: 21.7 us -> none  [per_device(): jnp.einsum('iak,jbk->ibja', masked_amps, weights, preferred_element_type=...]
    ppermute x0 -> x12, waiting for transfers between devices: none -> 14.7 us  [the longest x6 11.1 us: neighbours(): got.append(lax.ppermute(high, high_axis, ring(shift)))]
    reshape x1 -> x0, local copies, waits for them, and re-layouts: 7.34 us -> none  [per_device(): cycle = cycle.reshape(rows_here, pair_width, outer_count * V)]
    convert_element_type x1 -> x0, other arithmetic: 5.1 us -> none  [per_device(): return (residual.astype(jnp.float32) + cycle).astype(jnp.bfloat16)]
    unnamed x2 -> x0, local copies, waits for them, and re-layouts: 1.78 us -> none
  transfers between devices with their start and end apart: 2 -> 13, of which waited for: 2 -> 5; matrix products, arithmetic and copies ran while one was open for 1% -> 0% of each run, Pallas kernels for 0% -> 13%
where the time goes in v1:
time: 85.8 us; the launch traced here: 85.6 us
  starting transfers between devices  30.2 us (35%)
  Pallas kernels  22 us (26%)
  waiting for transfers between devices  14.7 us (17%)
  between operations  14.7 us (17%)
  local copies, waits for them, and re-layouts  1.77 us (2%)
  other arithmetic  1.51 us (2%)
    ppermute x6, starting transfers between devices, neighbours(): got.append(lax.ppermute(high, high_axis, ring(shift)))  22.5 us
    pallas_call x2, Pallas kernels, add_cycle(): pl.pallas_call(functools.partial(cycle_kernel, parts, 6 if width < V else...  13.8 us
    ppermute x6, waiting for transfers between devices, neighbours(): got.append(lax.ppermute(high, high_axis, ring(shift)))  11.1 us
    ppermute x6, starting transfers between devices, neighbours(): got.append(lax.ppermute(low, low_axis, ring(shift)))  7.61 us
    pallas_call x1, Pallas kernels, branch(): pl.pallas_call(functools.partial(fold_kernel, width), out_shape=[jax.Shap...  3.89 us
    pallas_call x1, Pallas kernels, stage(): pl.pallas_call(stage_kernel, out_shape=jax.ShapeDtypeStruct(residual.shap...  3.7 us
    ppermute x6, waiting for transfers between devices, neighbours(): got.append(lax.ppermute(low, low_axis, ring(shift)))  3.66 us
    cond x11, local copies, waits for them, and re-layouts  1.74 us
  transfers between devices with their start and end apart: 13, of which 5 were waited for; matrix products, arithmetic and copies ran while one was open for 0% of the time, Pallas kernels for 13%

profile of v1, /device:TPU:28, one launch (start us, length us, event | category | flops | bytes accessed | tf_op | source)
XLA Modules:
  0.0 85.6 jit_solution(8535612900854493885)
XLA Ops:
  6.5 0.1 pad_add_fusion
  6.6 1.4 %subtract_reduce_fusion = s32[]{:T(128)} fusion(s32[9]{0:T(128)} %param.15), kind=kLoop, calls=%fused_computation.25 | loop fusion | flops 15 | bytes 68 | tf_op jit(solution)/shard_map/reduce_max | solution.py:225
  9.4 69.4 %conditional.1 = (bf16[1,192,24576]{2,1,0:T(8,128)(2,1)}) conditional(s32[]{:T(128)} %clamp.3, (bf16[1,192,1536]{2,1,0:T(8,128)(2,1)}, bf16[1,192,1536]{2,1,0:T(8,128)(2,1)}, s32[4]{0:T(128)S(1)}, s32[9]{0:T(128)}, s32[1]{0:T(128)}, /*index=5*/s32[1]{0:T(128)}, s32[16]{0:T(128)}, bf16[1,192,24576]{2,1,0:T(8,128)(2,1)}) %tuple.23, ...), branch_computations={%region_1.2_spmd, %region_2.3_spmd, %region_3.4_spmd} | conditional | flops 14495514624 | bytes 131531792 | solution.py:230
  9.4 0.0 all-gather.6.cloned.1.call-start
  9.4 3.9 %fold.4 = (bf16[96,768]{1,0:T(8,128)(2,1)S(1)}, bf16[96,768]{1,0:T(8,128)(2,1)S(1)}, bf16[192,768]{1,0:T(8,128)(2,1)}) custom-call(s32[4]{0:T(128)S(1)} %get-tuple-element.86.where, s32[9]{0:T(128)} %get-tuple-element.87.offsets, s32[1]{0:T(128)} %get-tuple-element.150.inner, s32[1]{0:T(128)} %get-tuple-element.153.slab, s32[16]{0:T(128)} %get-tuple-element.156.outer, ...), custom_call_target="tpu_custom_call" | custom-call | tf_op jit(solution)/shard_map/cond/branch_1_fun/fold/pallas_call | solution.py:192
  13.3 0.0 all-gather.6.cloned.1.call-update
  13.3 4.0 %collective-permute-start.17 = (bf16[96,768]{1,0:T(8,128)(2,1)S(1)}, bf16[96,768]{1,0:T(8,128)(2,1)S(1)}, u32[]{:S(2)}, u32[]{:S(2)}) collective-permute-start(bf16[96,768]{1,0:T(8,128)(2,1)S(1)} %get-tuple-element.96), channel_id=1, source_target_pairs={{0,2},{1,3},{2,0},{3,1},{4,6},{5,7},{6,4},{7,5},{8,10},{9,11},{10,... | collective-permute-start | bytes 442376 | tf_op jit(solution)/shard_map/cond/branch_1_fun/ppermute | solution.py:183
  17.3 0.7 collective-permute-start.16
  18.0 1.3 %collective-permute-start.15 = (bf16[96,768]{1,0:T(8,128)(2,1)S(1)}, bf16[96,768]{1,0:T(8,128)(2,1)S(1)}, u32[]{:S(2)}, u32[]{:S(2)}) collective-permute-start(bf16[96,768]{1,0:T(8,128)(2,1)S(1)} %get-tuple-element.96), channel_id=1, source_target_pairs={{0,1},{1,2},{2,3},{3,0},{4,5},{5,6},{6,7},{7,4},{8,9},{9,10},{10,1... | collective-permute-start | bytes 442376 | tf_op jit(solution)/shard_map/cond/branch_1_fun/ppermute | solution.py:183
  19.3 0.5 collective-permute-start.14
  19.8 2.2 %collective-permute-start.13 = (bf16[96,768]{1,0:T(8,128)(2,1)S(1)}, bf16[96,768]{1,0:T(8,128)(2,1)S(1)}, u32[]{:S(2)}, u32[]{:S(2)}) collective-permute-start(bf16[96,768]{1,0:T(8,128)(2,1)S(1)} %get-tuple-element.97), channel_id=1, source_target_pairs={{0,12},{4,0},{8,4},{12,8},{1,13},{5,1},{9,5},{13,9},{2,14},{6,2},{... | collective-permute-start | bytes 442376 | tf_op jit(solution)/shard_map/cond/branch_1_fun/ppermute | solution.py:182
  22.0 0.0 collective-permute-done.17
  22.0 0.9 %collective-permute-start.12 = (bf16[96,768]{1,0:T(8,128)(2,1)S(1)}, bf16[96,768]{1,0:T(8,128)(2,1)S(1)}, u32[]{:S(2)}, u32[]{:S(2)}) collective-permute-start(bf16[96,768]{1,0:T(8,128)(2,1)S(1)} %get-tuple-element.97), channel_id=1, source_target_pairs={{0,4},{4,8},{8,12},{12,0},{1,5},{5,9},{9,13},{13,1},{2,6},{6,10},{... | collective-permute-start | bytes 442376 | tf_op jit(solution)/shard_map/cond/branch_1_fun/ppermute | solution.py:182
  22.9 2.2 %collective-permute-done.16 = bf16[96,768]{1,0:T(8,128)(2,1)S(1)} collective-permute-done((bf16[96,768]{1,0:T(8,128)(2,1)S(1)}, bf16[96,768]{1,0:T(8,128)(2,1)S(1)}, u32[]{:S(2)}, u32[]{:S(2)}) %collective-permute-start.16) | collective-permute-done | bytes 147488 | tf_op jit(solution)/shard_map/cond/branch_1_fun/ppermute | solution.py:183
  25.1 2.1 %collective-permute-done.14 = bf16[96,768]{1,0:T(8,128)(2,1)S(1)} collective-permute-done((bf16[96,768]{1,0:T(8,128)(2,1)S(1)}, bf16[96,768]{1,0:T(8,128)(2,1)S(1)}, u32[]{:S(2)}, u32[]{:S(2)}) %collective-permute-start.14) | collective-permute-done | bytes 147488 | tf_op jit(solution)/shard_map/cond/branch_1_fun/ppermute | solution.py:182
  27.2 0.6 collective-permute-done.13
  27.8 0.9 %collective-permute-done.12 = bf16[96,768]{1,0:T(8,128)(2,1)S(1)} collective-permute-done((bf16[96,768]{1,0:T(8,128)(2,1)S(1)}, bf16[96,768]{1,0:T(8,128)(2,1)S(1)}, u32[]{:S(2)}, u32[]{:S(2)}) %collective-permute-start.12) | collective-permute-done | bytes 147488 | tf_op jit(solution)/shard_map/cond/branch_1_fun/ppermute | solution.py:182
  28.8 0.6 collective-permute-start.23
  29.4 2.7 %collective-permute-start.22 = (bf16[384,768]{1,0:T(8,128)(2,1)S(1)}, bf16[384,768]{1,0:T(8,128)(2,1)S(1)}, u32[]{:S(2)}, u32[]{:S(2)}) collective-permute-start(bf16[384,768]{1,0:T(8,128)(2,1)S(1)} %constant_dynamic-update-slice_fusion.8.refs_1_), channel_id=1, source_target_pairs={{0,8},{4,12},{8,0},{12,4},{1,9},{5,13},{9,1},{13,5},{2,10},{6,14},... | collective-permute-start | bytes 1769480 | tf_op jit(solution)/shard_map/cond/branch_1_fun/ppermute | solution.py:183
  32.2 1.1 %collective-permute-start.21 = (bf16[384,768]{1,0:T(8,128)(2,1)S(1)}, bf16[384,768]{1,0:T(8,128)(2,1)S(1)}, u32[]{:S(2)}, u32[]{:S(2)}) collective-permute-start(bf16[384,768]{1,0:T(8,128)(2,1)S(1)} %constant_dynamic-update-slice_fusion.12.refs_0_), channel_id=1, source_target_pairs={{0,1},{1,2},{2,3},{3,0},{4,5},{5,6},{6,7},{7,4},{8,9},{9,10},{10,1... | collective-permute-start | bytes 1769480 | tf_op jit(solution)/shard_map/cond/branch_1_fun/ppermute | solution.py:182
  33.3 2.2 %collective-permute-start.20 = (bf16[384,768]{1,0:T(8,128)(2,1)S(1)}, bf16[384,768]{1,0:T(8,128)(2,1)S(1)}, u32[]{:S(2)}, u32[]{:S(2)}) collective-permute-start(bf16[384,768]{1,0:T(8,128)(2,1)S(1)} %constant_dynamic-update-slice_fusion.12.refs_0_), channel_id=1, source_target_pairs={{0,3},{1,0},{2,1},{3,2},{4,7},{5,4},{6,5},{7,6},{8,11},{9,8},{10,9... | collective-permute-start | bytes 1769480 | tf_op jit(solution)/shard_map/cond/branch_1_fun/ppermute | solution.py:182
  35.5 0.7 collective-permute-start.19
  36.2 8.9 %collective-permute-done.23.refs_3_ = bf16[384,768]{1,0:T(8,128)(2,1)S(1)} collective-permute-done((bf16[384,768]{1,0:T(8,128)(2,1)S(1)}, bf16[384,768]{1,0:T(8,128)(2,1)S(1)}, u32[]{:S(2)}, u32[]{:S(2)}) %collective-permute-start.23) | collective-permute-done | bytes 589856 | tf_op jit(solution)/shard_map/cond/branch_1_fun/ppermute | solution.py:183
  45.1 13.2 %collective-permute-start.18 = (bf16[384,768]{1,0:T(8,128)(2,1)S(1)}, bf16[384,768]{1,0:T(8,128)(2,1)}, u32[]{:S(2)}, u32[]{:S(2)}) collective-permute-start(bf16[384,768]{1,0:T(8,128)(2,1)S(1)} %constant_dynamic-update-slice_fusion.8.refs_1_), channel_id=1, source_target_pairs={{0,4},{4,8},{8,12},{12,0},{1,5},{5,9},{9,13},{13,1},{2,6},{6,10},{... | collective-permute-start | bytes 1769480 | tf_op jit(solution)/shard_map/cond/branch_1_fun/ppermute | solution.py:183
  58.3 1.7 %copy-done.1 = bf16[1536,768]{1,0:T(8,128)(2,1)S(1)} copy-done((bf16[1536,768]{1,0:T(8,128)(2,1)S(1)}, bf16[1536,768]{1,0:T(8,128)(2,1)}, u32[]{:S(2)}) %copy-start.1) | copy-done | bytes 2359320 | tf_op jit(solution)/shard_map/cond
  60.0 0.7 flip.4.amps
  60.6 0.0 copy-start.5
  60.7 0.0 copy-start.8
  60.7 3.7 %stage.4.refs_4_ = bf16[192,24576]{1,0:T(8,128)(2,1)S(1)} custom-call(bf16[192,24576]{1,0:T(8,128)(2,1)} %bitcast.17), custom_call_target="tpu_custom_call" | custom-call | tf_op jit(solution)/shard_map/cond/branch_1_fun/stage/pallas_call | solution.py:80
  64.4 6.5 %add_cycle.8.refs_5_ = bf16[192,24576]{1,0:T(8,128)(2,1)} custom-call(s32[4]{0:T(128)S(1)} %get-tuple-element.86.where, s32[9]{0:T(128)S(1)} %copy-done.5, s32[1]{0:T(128)} %get-tuple-element.153.slab, s32[16]{0:T(128)S(1)} %copy-done.8, bf16[768,1536]{1,0:T(8,128)(2,1)S(1)} %flip.4.amps, bf16[384,768]{1,0:T(8,128)(2,1)S(1)} %constant_dynamic-update-slice_fusion.12.refs_0_, ...), custom_call_target="tpu_custom_call" | custom-call | flops 3623878656 | bytes 9437184 | tf_op jit(solution)/shard_map/cond/branch_1_fun/add_cycle/pallas_call | solution.py:153
  70.9 0.0 collective-permute-done.20.refs_2_
  71.0 7.2 %add_cycle.9 = bf16[192,24576]{1,0:T(8,128)(2,1)} custom-call(s32[4]{0:T(128)S(1)} %get-tuple-element.86.where, s32[9]{0:T(128)S(1)} %copy-done.5, s32[1]{0:T(128)} %get-tuple-element.153.slab, s32[16]{0:T(128)S(1)} %copy-done.8, bf16[768,1536]{1,0:T(8,128)(2,1)S(1)} %flip.4.amps, ...), custom_call_target="tpu_custom_call", output_to_operand_aliasing={{}: (10, {})} | custom-call | flops 3623878656 | bytes 9437184 | tf_op jit(solution)/shard_map/cond/branch_1_fun/add_cycle/pallas_call | solution.py:153
  (16 shorter events, 0.1 us)
Async XLA Ops:
  9.4 48.9 %all-gather.6.cloned.1.call-start = ((), (), s32[]{:S(2)}) async-start(), calls=%async_computation.1 | async-start | bytes 2654208 | tf_op jit(solution)/shard_map/cond/branch_1_fun/all_gather | solution.py:202
  13.3 8.6 %collective-permute-start.17 = (bf16[96,768]{1,0:T(8,128)(2,1)S(1)}, bf16[96,768]{1,0:T(8,128)(2,1)S(1)}, u32[]{:S(2)}, u32[]{:S(2)}) collective-permute-start(bf16[96,768]{1,0:T(8,128)(2,1)S(1)} %get-tuple-element.96), channel_id=1, source_target_pairs={{0,2},{1,3},{2,0},{3,1},{4,6},{5,7},{6,4},{7,5},{8,10},{9,11},{10,... | collective-permute-start | bytes 442376 | tf_op jit(solution)/shard_map/cond/branch_1_fun/ppermute | solution.py:183
  17.3 7.8 %collective-permute-start.16 = (bf16[96,768]{1,0:T(8,128)(2,1)S(1)}, bf16[96,768]{1,0:T(8,128)(2,1)S(1)}, u32[]{:S(2)}, u32[]{:S(2)}) collective-permute-start(bf16[96,768]{1,0:T(8,128)(2,1)S(1)} %get-tuple-element.96), channel_id=1, source_target_pairs={{0,3},{1,0},{2,1},{3,2},{4,7},{5,4},{6,5},{7,6},{8,11},{9,8},{10,9... | collective-permute-start | bytes 442376 | tf_op jit(solution)/shard_map/cond/branch_1_fun/ppermute | solution.py:183
  18.0 7.1 %collective-permute-start.15 = (bf16[96,768]{1,0:T(8,128)(2,1)S(1)}, bf16[96,768]{1,0:T(8,128)(2,1)S(1)}, u32[]{:S(2)}, u32[]{:S(2)}) collective-permute-start(bf16[96,768]{1,0:T(8,128)(2,1)S(1)} %get-tuple-element.96), channel_id=1, source_target_pairs={{0,1},{1,2},{2,3},{3,0},{4,5},{5,6},{6,7},{7,4},{8,9},{9,10},{10,1... | collective-permute-start | bytes 442376 | tf_op jit(solution)/shard_map/cond/branch_1_fun/ppermute | solution.py:183
  19.3 7.9 %collective-permute-start.14 = (bf16[96,768]{1,0:T(8,128)(2,1)S(1)}, bf16[96,768]{1,0:T(8,128)(2,1)S(1)}, u32[]{:S(2)}, u32[]{:S(2)}) collective-permute-start(bf16[96,768]{1,0:T(8,128)(2,1)S(1)} %get-tuple-element.97), channel_id=1, source_target_pairs={{0,8},{4,12},{8,0},{12,4},{1,9},{5,13},{9,1},{13,5},{2,10},{6,14},... | collective-permute-start | bytes 442376 | tf_op jit(solution)/shard_map/cond/branch_1_fun/ppermute | solution.py:182
  19.8 8.0 %collective-permute-start.13 = (bf16[96,768]{1,0:T(8,128)(2,1)S(1)}, bf16[96,768]{1,0:T(8,128)(2,1)S(1)}, u32[]{:S(2)}, u32[]{:S(2)}) collective-permute-start(bf16[96,768]{1,0:T(8,128)(2,1)S(1)} %get-tuple-element.97), channel_id=1, source_target_pairs={{0,12},{4,0},{8,4},{12,8},{1,13},{5,1},{9,5},{13,9},{2,14},{6,2},{... | collective-permute-start | bytes 442376 | tf_op jit(solution)/shard_map/cond/branch_1_fun/ppermute | solution.py:182
  22.0 6.7 %collective-permute-start.12 = (bf16[96,768]{1,0:T(8,128)(2,1)S(1)}, bf16[96,768]{1,0:T(8,128)(2,1)S(1)}, u32[]{:S(2)}, u32[]{:S(2)}) collective-permute-start(bf16[96,768]{1,0:T(8,128)(2,1)S(1)} %get-tuple-element.97), channel_id=1, source_target_pairs={{0,4},{4,8},{8,12},{12,0},{1,5},{5,9},{9,13},{13,1},{2,6},{6,10},{... | collective-permute-start | bytes 442376 | tf_op jit(solution)/shard_map/cond/branch_1_fun/ppermute | solution.py:182
  28.8 16.3 %collective-permute-start.23 = (bf16[384,768]{1,0:T(8,128)(2,1)S(1)}, bf16[384,768]{1,0:T(8,128)(2,1)S(1)}, u32[]{:S(2)}, u32[]{:S(2)}) collective-permute-start(bf16[384,768]{1,0:T(8,128)(2,1)S(1)} %constant_dynamic-update-slice_fusion.8.refs_1_), channel_id=1, source_target_pairs={{0,12},{4,0},{8,4},{12,8},{1,13},{5,1},{9,5},{13,9},{2,14},{6,2},{... | collective-permute-start | bytes 1769480 | tf_op jit(solution)/shard_map/cond/branch_1_fun/ppermute | solution.py:183
  29.4 35.0 %collective-permute-start.22 = (bf16[384,768]{1,0:T(8,128)(2,1)S(1)}, bf16[384,768]{1,0:T(8,128)(2,1)S(1)}, u32[]{:S(2)}, u32[]{:S(2)}) collective-permute-start(bf16[384,768]{1,0:T(8,128)(2,1)S(1)} %constant_dynamic-update-slice_fusion.8.refs_1_), channel_id=1, source_target_pairs={{0,8},{4,12},{8,0},{12,4},{1,9},{5,13},{9,1},{13,5},{2,10},{6,14},... | collective-permute-start | bytes 1769480 | tf_op jit(solution)/shard_map/cond/branch_1_fun/ppermute | solution.py:183
  32.2 38.8 %collective-permute-start.21 = (bf16[384,768]{1,0:T(8,128)(2,1)S(1)}, bf16[384,768]{1,0:T(8,128)(2,1)S(1)}, u32[]{:S(2)}, u32[]{:S(2)}) collective-permute-start(bf16[384,768]{1,0:T(8,128)(2,1)S(1)} %constant_dynamic-update-slice_fusion.12.refs_0_), channel_id=1, source_target_pairs={{0,1},{1,2},{2,3},{3,0},{4,5},{5,6},{6,7},{7,4},{8,9},{9,10},{10,1... | collective-permute-start | bytes 1769480 | tf_op jit(solution)/shard_map/cond/branch_1_fun/ppermute | solution.py:182
  33.3 37.7 %collective-permute-start.20 = (bf16[384,768]{1,0:T(8,128)(2,1)S(1)}, bf16[384,768]{1,0:T(8,128)(2,1)S(1)}, u32[]{:S(2)}, u32[]{:S(2)}) collective-permute-start(bf16[384,768]{1,0:T(8,128)(2,1)S(1)} %constant_dynamic-update-slice_fusion.12.refs_0_), channel_id=1, source_target_pairs={{0,3},{1,0},{2,1},{3,2},{4,7},{5,4},{6,5},{7,6},{8,11},{9,8},{10,9... | collective-permute-start | bytes 1769480 | tf_op jit(solution)/shard_map/cond/branch_1_fun/ppermute | solution.py:182
  35.5 35.5 %collective-permute-start.19 = (bf16[384,768]{1,0:T(8,128)(2,1)S(1)}, bf16[384,768]{1,0:T(8,128)(2,1)}, u32[]{:S(2)}, u32[]{:S(2)}) collective-permute-start(bf16[384,768]{1,0:T(8,128)(2,1)S(1)} %constant_dynamic-update-slice_fusion.12.refs_0_), channel_id=1, source_target_pairs={{0,2},{1,3},{2,0},{3,1},{4,6},{5,7},{6,4},{7,5},{8,10},{9,11},{10,... | collective-permute-start | bytes 1769480 | tf_op jit(solution)/shard_map/cond/branch_1_fun/ppermute | solution.py:182
  45.1 25.8 %collective-permute-start.18 = (bf16[384,768]{1,0:T(8,128)(2,1)S(1)}, bf16[384,768]{1,0:T(8,128)(2,1)}, u32[]{:S(2)}, u32[]{:S(2)}) collective-permute-start(bf16[384,768]{1,0:T(8,128)(2,1)S(1)} %constant_dynamic-update-slice_fusion.8.refs_1_), channel_id=1, source_target_pairs={{0,4},{4,8},{8,12},{12,0},{1,5},{5,9},{9,13},{13,1},{2,6},{6,10},{... | collective-permute-start | bytes 1769480 | tf_op jit(solution)/shard_map/cond/branch_1_fun/ppermute | solution.py:183
  58.3 1.7 %copy-start.1 = (bf16[1536,768]{1,0:T(8,128)(2,1)S(1)}, bf16[1536,768]{1,0:T(8,128)(2,1)}, u32[]{:S(2)}) copy-start(bf16[1536,768]{1,0:T(8,128)(2,1)} %all-gather.6.cloned.1.call-done.source) | copy-start | bytes 7077892 | tf_op jit(solution)/shard_map/cond
  60.6 3.7 %copy-start.5 = (s32[9]{0:T(128)S(1)}, s32[9]{0:T(128)}, u32[]{:S(2)}) copy-start(s32[9]{0:T(128)} %get-tuple-element.87.offsets) | copy-start | bytes 112 | tf_op jit(solution)/shard_map/cond
  60.7 3.7 %copy-start.8 = (s32[16]{0:T(128)S(1)}, s32[16]{0:T(128)}, u32[]{:S(2)}) copy-start(s32[16]{0:T(128)} %get-tuple-element.156.outer) | copy-start | bytes 196 | tf_op jit(solution)/shard_map/cond
Sparse Core Ops, SparseCore 0:
  13.5 26.5 all-gather.5
